TPU v7x, 32 devices: a whole 2x2x4 slice. The times are simulated.
32 devices in a mesh: groups: 1, dp: 32 (over z, y, x, core).
Axes of the slice: x: 2, y: 2, z: 4, core: 2. Of those that a mesh axis runs over, the one named last changes fastest.
Arguments:
- queries: bfloat16 [4096, 4096], P(('groups', 'dp')), may hold values from -9 to 9
- own_kv: bfloat16 [4096, 1024], P(('groups', 'dp')), may hold values from -6 to 6
- cotangent: bfloat16 [4096, 4096], P(('groups', 'dp')), may hold values from -6 to 6
- cartridges: bfloat16 [32, 768, 1024], P(('groups', 'dp')), may hold values from -6 to 6
- block_mask: int32 [32, 6], P(('groups', 'dp')), may hold values from 0 to 1, as said below
- owner: int32 [1], P('groups'), may hold values from 0 to 31
Outputs:
- update: float32 [768, 1024], P(('groups', 'dp'))
Inputs may be any that keep to these rules, and one draw needn't show every extreme that they name: block_mask[c, b] is 1 when conversation c may attend to slots b * 128 to b * 128 + 127, else 0.
All inputs are finite; a program needn't handle non-finite values.
Results may differ from a plain program's by a relative error of at most 0.0047.
Values may be sent and summed in bfloat16 or wider, within the bound.
A program may use at most 64 MiB of HBM per device.

v0:
```python
import jax
import jax.numpy as jnp
from jax import lax
from jax.sharding import PartitionSpec as P

HD = 128
QH = 32
KVH = 4
BLOCK = 128


masked_score = -1e30
norm_epsilon = 1e-06


def from_root(value, axis, source):
    kept = jnp.where(lax.axis_index(axis) == source, value, 0).astype(value.dtype)
    return lax.psum(kept, axis)


def head_terms(queries, grad_out, own_keys, own_values, cart_keys, cart_values, allowed, causal):
    score_scale = HD ** (-0.5)
    scores_cart = (
        jnp.einsum("clgd,sd->clgs", queries, cart_keys, preferred_element_type=jnp.float32)
        * score_scale
    )
    scores_own = (
        jnp.einsum("clgd,cud->clgu", queries, own_keys, preferred_element_type=jnp.float32)
        * score_scale
    )
    scores_cart = jnp.where(allowed[:, None, None, :], scores_cart, masked_score)
    scores_own = jnp.where(causal[None, :, None, :], scores_own, masked_score)
    row_max = jnp.maximum(jnp.max(scores_cart, axis=3), jnp.max(scores_own, axis=3))[..., None]
    exp_cart = jnp.exp(scores_cart - row_max)
    exp_own = jnp.exp(scores_own - row_max)
    row_sum = jnp.sum(exp_cart, axis=3, keepdims=True) + jnp.sum(exp_own, axis=3, keepdims=True)
    prob_cart = exp_cart / row_sum
    prob_own = exp_own / row_sum
    low_cart = prob_cart.astype(jnp.bfloat16)
    low_own = prob_own.astype(jnp.bfloat16)
    attended = jnp.einsum(
        "clgs,sd->clgd", low_cart, cart_values, preferred_element_type=jnp.float32
    )
    attended = attended + jnp.einsum(
        "clgu,cud->clgd", low_own, own_values, preferred_element_type=jnp.float32
    )
    grad_prob = jnp.einsum(
        "clgd,sd->clgs", grad_out, cart_values, preferred_element_type=jnp.float32
    )
    row_dot = jnp.sum(grad_out.astype(jnp.float32) * attended, axis=3, keepdims=True)
    grad_score = (prob_cart * (grad_prob - row_dot)).astype(jnp.bfloat16)
    grad_keys = (
        jnp.einsum("clgs,clgd->sd", grad_score, queries, preferred_element_type=jnp.float32)
        * score_scale
    )
    grad_values = jnp.einsum(
        "clgs,clgd->sd", low_cart, grad_out, preferred_element_type=jnp.float32
    )
    return (grad_keys, grad_values)


def body(queries, own_kv, cotangent, cartridges, block_mask, owner):
    conv_dev = block_mask.shape[0]
    seq_len = queries.shape[0] // conv_dev
    slot_count = cartridges.shape[1]
    half_width = KVH * HD
    groups_q = QH // KVH
    owner_index = owner[0]
    local_cart = cartridges[0]
    whole_cart = from_root(local_cart, "dp", owner_index)
    cart_keys = whole_cart[:, :half_width]
    cart_values = whole_cart[:, half_width:]
    query_heads = queries.reshape(conv_dev, seq_len, KVH, groups_q, HD)
    grad_heads = cotangent.reshape(conv_dev, seq_len, KVH, groups_q, HD)
    own_heads = own_kv.reshape(conv_dev, seq_len, 2, KVH, HD)
    key_heads = cart_keys.reshape(slot_count, KVH, HD)
    value_heads = cart_values.reshape(slot_count, KVH, HD)
    allowed = jnp.repeat(block_mask > 0, BLOCK, axis=1)
    positions = jnp.arange(seq_len)
    causal = positions[:, None] >= positions[None, :]
    key_parts = []
    value_parts = []
    for kv_head in range(KVH):
        keys_part, values_part = head_terms(
            query_heads[:, :, kv_head],
            grad_heads[:, :, kv_head],
            own_heads[:, :, 0, kv_head],
            own_heads[:, :, 1, kv_head],
            key_heads[:, kv_head],
            value_heads[:, kv_head],
            allowed,
            causal,
        )
        key_parts.append(keys_part)
        value_parts.append(values_part)
    local_grad = jnp.concatenate(key_parts + value_parts, axis=1)
    width_total = local_grad.shape[1]
    own_rows = lax.psum_scatter(local_grad, "dp", scatter_dimension=0, tiled=True)
    squares = lax.psum(jnp.sum(own_rows * own_rows), "dp")
    return own_rows / jnp.sqrt(squares / (slot_count * width_total) + norm_epsilon)


def solution(mesh):
    return jax.shard_map(
        body,
        mesh=mesh,
        in_specs=(
            P(("groups", "dp"), None),
            P(("groups", "dp"), None),
            P(("groups", "dp"), None),
            P(("groups", "dp"), None, None),
            P(("groups", "dp"), None),
            P("groups"),
        ),
        out_specs=P(("groups", "dp"), None),
        check_vma=False,
    )
```

profile of v0, /device:TPU:0, one launch (start us, length us, event | category | flops | bytes accessed | tf_op | source)
XLA Modules:
  0.0 350.7 jit_solution(18135412900798111708)
XLA Ops:
  7.2 1.7 copy.171
  9.0 1.3 select_bitcast_fusion
  10.3 0.2 copy.175
  10.5 0.3 copy-done.10
  10.8 0.7 copy.173
  11.5 2.0 copy.178
  13.5 0.1 fusion.113
  13.6 1.1 fusion.114
  14.8 0.9 copy.293
  15.7 0.9 copy.288
  16.5 0.8 copy.283
  17.4 0.9 copy.278
  18.2 1.1 fusion.116
  19.3 1.1 fusion.117
  20.4 1.1 fusion.115
  21.5 125.9 %all-reduce.2.cloned.1.call-done = bf16[768,1024]{0,1:T(8,128)(2,1)} async-done(((bf16[768,1024]{0,1:T(8,128)(2,1)}), bf16[768,1024]{0,1:T(8,128)(2,1)}) %all-reduce.2.cloned.1.call-update) | async-done | bytes 1572880 | tf_op jit(solution)/shard_map/psum | solution.py:18
  147.4 1.5 fusion.112
  148.9 0.6 fusion.86
  149.5 1.8 fusion.84
  151.3 0.4 copy-done.5
  151.8 1.1 bitcast_reduce_fusion
  152.9 0.1 fusion.60
  153.0 0.1 fusion.63
  153.1 2.5 fusion.15
  155.8 0.1 fusion.62
  155.9 1.9 fusion.13
  157.8 2.0 fusion.55
  159.9 2.0 fusion.52
  161.9 2.0 fusion.49
  163.9 1.2 fusion.58
  165.1 0.4 fusion.47
  165.5 3.5 fusion.33
  169.0 1.8 fusion.46
  170.8 1.7 fusion.45
  172.5 0.4 fusion.44
  172.9 4.5 %fusion.35 = f32[768,1024]{0,1:T(8,128)} fusion(f32[768,1024]{0,1:T(8,128)} %fusion.33, f32[128,8]{0,1:T(8,128)S(1)} %fusion.46, bf16[1,128,4,8,128]{1,4,3,2,0:T(8,128)(2,1)} %bitcast.386, bf16[768,4,128]{0,2,1:T(8,128)(2,1)} %bitcast.400, bf16[1,128,4,8,128]{1,4,3,2,0:T(8,128)(2,1)} %bitcast.372, f32[768,128,8]{1,0,2:T(8,128)} %copy-done.8, ...), kind=kOutput, calls=%fused_computation.60 | convolution fusion | flops 408256512 | bytes 4272896 | tf_op jit(solution)/shard_map/clgs,clgd->sd/dot_general | solution.py:53
  177.4 4.4 %fusion.37 = f32[768,1024]{0,1:T(8,128)} fusion(f32[768,1024]{0,1:T(8,128)} %fusion.35, f32[128,8]{0,1:T(8,128)S(1)} %fusion.45, bf16[1,128,4,8,128]{1,4,3,2,0:T(8,128)(2,1)} %bitcast.387, bf16[768,4,128]{0,2,1:T(8,128)(2,1)} %bitcast.401, bf16[1,128,4,8,128]{1,4,3,2,0:T(8,128)(2,1)} %bitcast.373, f32[768,128,8]{1,0,2:T(8,128)} %copy-done, ...), kind=kOutput, calls=%fused_computation.62 | convolution fusion | flops 408256512 | bytes 4272896 | tf_op jit(solution)/shard_map/clgs,clgd->sd/dot_general | solution.py:53
  181.8 4.5 %fusion.39 = f32[768,1024]{0,1:T(8,128)} fusion(f32[768,1024]{0,1:T(8,128)} %fusion.37, f32[128,8]{0,1:T(8,128)S(1)} %fusion.44, bf16[1,128,4,8,128]{1,4,3,2,0:T(8,128)(2,1)} %bitcast.388, bf16[768,4,128]{0,2,1:T(8,128)(2,1)} %bitcast.402, bf16[1,128,4,8,128]{1,4,3,2,0:T(8,128)(2,1)} %bitcast.374, f32[768,128,8]{1,0,2:T(8,128)} %copy-done.6, ...), kind=kOutput, calls=%fused_computation.64 | convolution fusion | flops 408256512 | bytes 4272896 | tf_op jit(solution)/shard_map/clgs,clgd->sd/dot_general | solution.py:53
  186.3 3.2 fusion.43
  189.5 1.9 fusion.42
  191.5 1.9 fusion.41
  193.4 2.0 fusion.40
  195.4 3.5 %copy.272 = f32[768,1024]{1,0:T(8,128)} copy(f32[768,1024]{0,1:T(8,128)} %fusion.40) | data formatting | bytes 6291456
  198.9 100.6 %reduce-scatter.4.cloned.1.call-done = f32[24,1024]{1,0:T(8,128)} async-done(((f32[768,1024]{1,0:T(8,128)}), f32[24,1024]{1,0:T(8,128)}) %reduce-scatter.4.cloned.1.call-update) | async-done | bytes 98320 | tf_op jit(solution)/shard_map/reduce_scatter | solution.py:98
  299.5 1.1 copy.273
  300.6 0.7 multiply_reduce_fusion
  301.3 40.2 %psum.15 = f32[]{:T(128)} all-reduce(f32[]{:T(128)} %multiply_reduce_fusion), channel_id=1, replica_groups=mesh['groups'=1,'dp'=32] {'dp'}, use_global_device_ids=true, to_apply=%region_23.24 | all-reduce | flops 1 | bytes 8 | tf_op jit(solution)/shard_map/psum | solution.py:99
  342.3 1.5 broadcast_divide_fusion
  (58 shorter events, 0.4 us)
Async XLA Ops:
  6.5 140.9 %all-reduce.2.cloned.1.call-start = ((), (), s32[]{:S(2)}) async-start(), calls=%async_computation.1 | async-start | bytes 3145728 | tf_op jit(solution)/shard_map/psum | solution.py:18
  8.9 1.4 copy-start.20
  8.9 1.4 copy-start.17
  8.9 1.9 copy-start.10
  10.2 289.3 %reduce-scatter.4.cloned.1.call-start = ((), (), s32[]{:S(2)}) async-start(), calls=%async_computation.2 | async-start | bytes 3244032 | tf_op jit(solution)/shard_map/reduce_scatter | solution.py:98
  11.5 137.4 %copy-start.4 = (bf16[128,4096]{0,1:T(8,128)(2,1)}, bf16[128,4096]{0,1:T(8,128)(2,1)S(1)}, u32[]{:S(2)}) copy-start(bf16[128,4096]{0,1:T(8,128)(2,1)S(1)} %copy.173) | copy-start | bytes 3145732
  13.5 6.9 %copy-start.2 = (bf16[128,4096]{0,1:T(8,128)(2,1)}, bf16[128,4096]{0,1:T(8,128)(2,1)S(1)}, u32[]{:S(2)}) copy-start(bf16[128,4096]{0,1:T(8,128)(2,1)S(1)} %copy.178) | copy-start | bytes 3145732
  148.9 15.0 %copy-start.11 = (bf16[768,512]{0,1:T(8,128)(2,1)}, bf16[768,512]{0,1:T(8,128)(2,1)S(1)}, u32[]{:S(2)}) copy-start(bf16[768,512]{0,1:T(8,128)(2,1)S(1)} %get-tuple-element.14) | copy-start | bytes 2359300
  149.5 10.4 %copy-start = (f32[768,128,8]{1,0,2:T(8,128)}, f32[768,128,8]{1,0,2:T(8,128)S(1)}, u32[]{:S(2)}) copy-start(f32[768,128,8]{1,0,2:T(8,128)S(1)} %fusion.86) | copy-start | bytes 9437188
  149.5 2.3 copy-start.5
  151.8 1.1 copy-start.16
  151.8 1.2 copy-start.12
  152.9 9.0 %copy-start.6 = (f32[768,128,8]{1,0,2:T(8,128)}, f32[768,128,8]{1,0,2:T(8,128)S(1)}, u32[]{:S(2)}) copy-start(f32[768,128,8]{1,0,2:T(8,128)S(1)} %get-tuple-element.19) | copy-start | bytes 9437188
  153.1 2.6 copy-start.15
  153.1 2.7 copy-start.14
  155.7 2.2 copy-start.8
  163.9 1.2 copy-start.19
  169.0 3.5 copy-start.13
  169.0 3.5 copy-start.18
  169.0 3.5 copy-start.21
  186.3 3.3 copy-start.3
  186.3 3.3 copy-start.9
  189.5 2.0 copy-start.1
  191.5 1.9 copy-start.7
Sparse Core Ops, SparseCore 0:
  12.6 134.7 all-reduce.1
  199.1 100.3 reduce-scatter.3
where the time goes:
time: 351 us
  waiting for transfers between devices  227 us (65%)
  matrix products  47.8 us (14%)
  blocking collectives  40.2 us (11%)
  between operations  15.2 us (4%)
  local copies, waits for them, and re-layouts  15.1 us (4%)
  other arithmetic  5.84 us (2%)
    psum x1, waiting for transfers between devices, from_root(): return lax.psum(kept, axis)  126 us
    reduce_scatter x1, waiting for transfers between devices, body(): lax.psum_scatter(local_grad, 'dp', scatter_dimension=0, tiled=True)  101 us
    psum x1, blocking collectives, body(): squares = lax.psum(jnp.sum(own_rows * own_rows), 'dp')  40.2 us
    dot_general x4, matrix products, head_terms(): jnp.einsum('clgs,clgd->sd', grad_score, queries, preferred_element_type=j...  16.8 us
    unnamed x54, local copies, waits for them, and re-layouts  13.4 us
    dot_general x4, matrix products, head_terms(): jnp.einsum('clgs,clgd->sd', low_cart, grad_out, preferred_element_type=jn...  9.1 us
    dot_general x4, matrix products, head_terms(): jnp.einsum('clgs,sd->clgd', low_cart, cart_values, preferred_element_type...  7.21 us
  transfers between devices with their start and end apart: 2, of which 2 were waited for; matrix products, arithmetic and copies ran while one was open for 3% of the time, Pallas kernels for 0%

commit v1 on v0

--- a/solution.py
+++ b/solution.py
@@ -1,6 +1,8 @@
 import jax
 import jax.numpy as jnp
 from jax import lax
+from jax.experimental import pallas as pl
+from jax.experimental.pallas import tpu as pltpu
 from jax.sharding import PartitionSpec as P
 
 HD = 128
@@ -100,9 +102,260 @@
     return own_rows / jnp.sqrt(squares / (slot_count * width_total) + norm_epsilon)
 
 
+SCALE = HD ** (-0.5)
+LOG2E = 1.4426950408889634
+
+
+def attend(j, q_ref, kv_ref, ct_ref, bias_ref, cart, kk, vv, grad):
+    slots = SLOTS_PER
+    half = KVH * HD
+    kk[:slots] = cart[j, :, :, :, 0].reshape(slots, HD)
+    vv[:slots] = cart[j, :, :, :, 1].reshape(slots, HD)
+    kk[slots:] = kv_ref[:, j * HD:(j + 1) * HD]
+    vv[slots:] = kv_ref[:, half + j * HD:half + (j + 1) * HD]
+    groups = QH // KVH
+    grad[j] = jnp.zeros_like(grad[j])
+
+    def pair(i, carry):
+        base = j * groups * HD + i * 2 * HD
+        one = pl.ds(pl.multiple_of(base, HD), HD)
+        two = pl.ds(pl.multiple_of(base + HD, HD), HD)
+        q = jnp.concatenate([q_ref[:, one], q_ref[:, two]], axis=0)
+        ct = jnp.concatenate([ct_ref[:, one], ct_ref[:, two]], axis=0)
+        nt = (((1,), (1,)), ((), ()))
+        scores = lax.dot_general(kk[...], q, nt, preferred_element_type=jnp.float32)
+        x = scores * (SCALE * LOG2E) + bias_ref[...]
+        e = jnp.exp2(x - jnp.max(x, axis=0, keepdims=True))
+        prob = e * (1.0 / jnp.sum(e, axis=0, keepdims=True))
+        low = prob.astype(jnp.bfloat16)
+        gp = lax.dot_general(vv[...], ct, nt, preferred_element_type=jnp.float32)
+        row_dot = jnp.sum(low.astype(jnp.float32) * gp, axis=0, keepdims=True)
+        gs = (prob[:slots] * (gp[:slots] - row_dot)).astype(jnp.bfloat16)
+        grad[j, :, :HD] += jnp.dot(gs, q, preferred_element_type=jnp.float32)
+        grad[j, :, HD:] += jnp.dot(low[:slots], ct, preferred_element_type=jnp.float32)
+        return carry
+
+    lax.fori_loop(0, groups // 2, pair, 0)
+    grad[j, :, :HD] = grad[j, :, :HD] * SCALE
+
+
+SLOTS_PER = 768
+SEG = (24, 2 * HD)
+N_SEM = 21 * KVH + 7
+
+
+def kernel(q_ref, kv_ref, ct_ref, bias_ref, w_ref, out_ref,
+           cart, rc, a1, rx, a2, rz, kk, vv, grad,
+           gc, b1, sx, gx, b2, gz, own, sq, sqr, send_sem, recv_sem):
+    me = lax.axis_index("dp")
+    core = me % 2
+    xy = (me // 2) % 4
+    zz = me // 8
+    bit = [me % 2, (me // 2) % 2, (me // 4) % 2, (me // 8) % 2, (me // 16) % 2]
+    flip = [1 - 2 * b for b in bit]
+
+    def moved(d, lo):
+        step = 0
+        if d & 1:
+            step = step + flip[lo]
+        if d & 2:
+            step = step + 2 * flip[lo + 1]
+        return step
+
+    core_peer = me + flip[0]
+    xy_step = {d: moved(d, 1) for d in (1, 2, 3)}
+    z_step = {d: moved(d, 3) for d in (1, 2, 3)}
+    xy_peer = {d: me + 2 * xy_step[d] for d in (1, 2, 3)}
+    z_peer = {d: me + 8 * z_step[d] for d in (1, 2, 3)}
+
+    barrier = pltpu.get_barrier_semaphore()
+    peers = [core_peer] + list(xy_peer.values()) + list(z_peer.values())
+    for peer in peers:
+        pl.semaphore_signal(barrier, inc=1, device_id={"dp": peer}, device_id_type=pl.DeviceIdType.MESH)
+    pl.semaphore_wait(barrier, len(peers))
+
+    sent = []
+    count = [0]
+
+    def send(src, dst, peer):
+        i = count[0]
+        count[0] += 1
+        copy = pltpu.make_async_remote_copy(
+            src_ref=src, dst_ref=dst, send_sem=send_sem.at[i], recv_sem=recv_sem.at[i],
+            device_id={"dp": peer}, device_id_type=pl.DeviceIdType.MESH)
+        copy.start()
+        sent.append(copy)
+        return copy
+
+    def head(j):
+        c = [send(w_ref.at[j, 1 - core], rc.at[j], core_peer)]
+        yield
+        c[0].wait_recv()
+        a1[j] = w_ref[j, core] + rc[j]
+        c = [send(a1.at[j, xy + xy_step[d]], rx.at[j, d - 1], xy_peer[d]) for d in (1, 2, 3)]
+        yield
+        for k in c:
+            k.wait_recv()
+        a2[j] = (a1[j, xy] + rx[j, 0]) + (rx[j, 1] + rx[j, 2])
+        c = []
+        for d in (1, 2, 3):
+            p = zz + z_step[d]
+            c.append(send(a2.at[j, p // 2, p % 2], rz.at[j, d - 1], z_peer[d]))
+        yield
+        for k in c:
+            k.wait_recv()
+        spot = cart.at[j, core, xy, zz // 2, zz % 2]
+        cart[j, core, xy, zz // 2, zz % 2] = (a2[j, zz // 2, zz % 2] + rz[j, 0]) + (rz[j, 1] + rz[j, 2])
+        c = [send(spot, spot, z_peer[d]) for d in (1, 2, 3)]
+        yield
+        for k in c:
+            k.wait_recv()
+        spot = cart.at[j, core, xy]
+        c = [send(spot, spot, xy_peer[d]) for d in (1, 2, 3)]
+        yield
+        for k in c:
+            k.wait_recv()
+        c = [send(cart.at[j, core], cart.at[j, core], core_peer)]
+        yield
+        c[0].wait_recv()
+        yield "compute"
+        attend(j, q_ref, kv_ref, ct_ref, bias_ref, cart, kk, vv, grad)
+        half = SLOTS_PER // 2
+        c = [send(grad.at[j, pl.ds(pl.multiple_of((1 - core) * half, 8), half)], gc.at[j], core_peer)]
+        yield
+        c[0].wait_recv()
+        b1[j] = (grad[j, pl.ds(pl.multiple_of(core * half, 8), half)] + gc[j]).reshape(4, half // 4, 2 * HD)
+        c = []
+        for d in (1, 2, 3):
+            sx[j, d - 1] = b1[j, xy + xy_step[d]].astype(jnp.bfloat16)
+            c.append(send(sx.at[j, d - 1], gx.at[j, d - 1], xy_peer[d]))
+        yield
+        for k in c:
+            k.wait_recv()
+        total = b1[j, xy]
+        for d in (1, 2, 3):
+            total = total + gx[j, d - 1].astype(jnp.float32)
+        b2[j] = total.reshape(4, SEG[0], SEG[1])
+        c = [send(b2.at[j, zz + z_step[d]], gz.at[j, d - 1], z_peer[d]) for d in (1, 2, 3)]
+        yield
+        for k in c:
+            k.wait_recv()
+        own[j] = (b2[j, zz] + gz[j, 0]) + (gz[j, 1] + gz[j, 2])
+
+    heads = [head(j) for j in range(KVH)]
+    started = 0
+    waiting = {}
+    tick = 0
+    live = []
+    while True:
+        if started < KVH:
+            live.append(started)
+            started += 1
+        if not live:
+            break
+        ready = None
+        for j in list(live):
+            if j in waiting:
+                continue
+            try:
+                got = next(heads[j])
+                if got == "compute":
+                    waiting[j] = True
+            except StopIteration:
+                live.remove(j)
+        if waiting:
+            j = min(waiting)
+            del waiting[j]
+            next(heads[j])
+        tick += 1
+
+    part = jnp.zeros((8, HD), jnp.float32)
+    for j in range(KVH):
+        v = own[j]
+        v = v * v
+        for r in range(0, SEG[0], 8):
+            for l in range(0, SEG[1], HD):
+                part = part + v[r:r + 8, l:l + HD]
+    sq[0] = part
+    c = send(sq.at[0], sqr.at[0], core_peer)
+    c.wait_recv()
+    sq[1] = sq[0] + sqr[0]
+    cs = [send(sq.at[1], sqr.at[d], xy_peer[d]) for d in (1, 2, 3)]
+    for k in cs:
+        k.wait_recv()
+    sq[2] = (sq[1] + sqr[1]) + (sqr[2] + sqr[3])
+    cs = [send(sq.at[2], sqr.at[3 + d], z_peer[d]) for d in (1, 2, 3)]
+    for k in cs:
+        k.wait_recv()
+    squares = jnp.sum((sq[2] + sqr[4]) + (sqr[5] + sqr[6]))
+    factor = 1.0 / jnp.sqrt(squares * jnp.ones((1, HD), jnp.float32) / (SLOTS_PER * 2 * KVH * HD) + norm_epsilon)
+    for j in range(KVH):
+        out_ref[:, j * HD:(j + 1) * HD] = own[j, :, :HD] * factor
+        out_ref[:, (KVH + j) * HD:(KVH + j + 1) * HD] = own[j, :, HD:] * factor
+    for k in sent:
+        k.wait_send()
+
+
+def fused(queries, own_kv, cotangent, cartridges, block_mask, owner):
+    slots, width = cartridges.shape[1:]
+    seq = queries.shape[0]
+    mine = jnp.where(lax.axis_index("dp") == owner[0], cartridges[0], 0).astype(jnp.bfloat16)
+    w = mine.reshape(4, 4, 2, 24, 2, KVH, HD).transpose(5, 2, 1, 0, 3, 4, 6)
+    w = w.reshape(KVH, 2, 4, 2, 48, 2, HD).transpose(0, 1, 2, 3, 5, 4, 6)
+    allowed = jnp.repeat(block_mask[0] > 0, BLOCK)
+    allowed = allowed.reshape(4, 4, 2, 24).transpose(2, 1, 0, 3).reshape(slots)
+    bias = jnp.broadcast_to(jnp.where(allowed, 0.0, masked_score)[:, None], (slots, 2 * seq))
+    pos = jnp.arange(seq)
+    causal = jnp.where(pos[:, None] <= jnp.tile(pos, 2)[None, :], 0.0, masked_score)
+    bias = jnp.concatenate([bias, causal], axis=0).astype(jnp.float32)
+    bf, f32 = jnp.bfloat16, jnp.float32
+    vm = pl.BlockSpec(memory_space=pltpu.VMEM)
+    piece = (48, HD)
+    return pl.pallas_call(
+        kernel,
+        out_shape=jax.ShapeDtypeStruct((24, width), f32),
+        in_specs=[vm] * 5,
+        out_specs=vm,
+        scratch_shapes=[
+            pltpu.VMEM((KVH, 2, 4, 2, 2) + piece, bf),
+            pltpu.VMEM((KVH, 4, 2, 2) + piece, bf),
+            pltpu.VMEM((KVH, 4, 2, 2) + piece, bf),
+            pltpu.VMEM((KVH, 3, 2, 2) + piece, bf),
+            pltpu.VMEM((KVH, 2, 2) + piece, bf),
+            pltpu.VMEM((KVH, 3) + piece, bf),
+            pltpu.VMEM((slots + seq, HD), bf),
+            pltpu.VMEM((slots + seq, HD), bf),
+            pltpu.VMEM((KVH, slots, 2 * HD), f32),
+            pltpu.VMEM((KVH, slots // 2, 2 * HD), f32),
+            pltpu.VMEM((KVH, 4, slots // 8, 2 * HD), f32),
+            pltpu.VMEM((KVH, 3, slots // 8, 2 * HD), bf),
+            pltpu.VMEM((KVH, 3, slots // 8, 2 * HD), bf),
+            pltpu.VMEM((KVH, 4) + SEG, f32),
+            pltpu.VMEM((KVH, 3) + SEG, f32),
+            pltpu.VMEM((KVH,) + SEG, f32),
+            pltpu.VMEM((3, 8, HD), f32),
+            pltpu.VMEM((7, 8, HD), f32),
+            pltpu.SemaphoreType.DMA((N_SEM,)),
+            pltpu.SemaphoreType.DMA((N_SEM,)),
+        ],
+        compiler_params=pltpu.CompilerParams(
+            collective_id=0, has_side_effects=True, vmem_limit_bytes=48 * 1024 * 1024),
+    )(queries, own_kv, cotangent, bias, w)
+
+
+def dispatch(size):
+    def run(queries, own_kv, cotangent, cartridges, block_mask, owner):
+        fits = (size == 32 and block_mask.shape == (1, 6)
+                and queries.shape == (128, QH * HD)
+                and cartridges.shape == (1, SLOTS_PER, 2 * KVH * HD))
+        chosen = fused if fits else body
+        return chosen(queries, own_kv, cotangent, cartridges, block_mask, owner)
+    return run
+
+
 def solution(mesh):
     return jax.shard_map(
-        body,
+        dispatch(mesh.shape["dp"]),
         mesh=mesh,
         in_specs=(
             P(("groups", "dp"), None),

time: 351 us -> 76.9 us (0.22)
  waiting for transfers between devices: 227 us -> 0 us
  Pallas kernels: 0 us -> 71.7 us
  matrix products: 47.8 us -> 0 us
  blocking collectives: 40.2 us -> 0 us
  between operations: 15.2 us -> 0.78 us
  local copies, waits for them, and re-layouts: 15.1 us -> 4.1 us
  other arithmetic: 5.84 us -> 0.31 us
    psum x1 -> x0, waiting for transfers between devices: 126 us -> none  [from_root(): return lax.psum(kept, axis)]
    reduce_scatter x1 -> x0, waiting for transfers between devices: 101 us -> none  [body(): lax.psum_scatter(local_grad, 'dp', scatter_dimension=0, tiled=True)]
    pallas_call x0 -> x1, Pallas kernels: none -> 71.7 us  [fused(): pl.pallas_call(kernel, out_shape=jax.ShapeDtypeStruct((24, width), f32),...]
    dot_general x24 -> x0, matrix products: 47.8 us -> none  [the longest x4 16.8 us: head_terms(): jnp.einsum('clgs,clgd->sd', grad_score, queries, preferred_element_type=j...]
    psum x1 -> x0, blocking collectives: 40.2 us -> none  [body(): squares = lax.psum(jnp.sum(own_rows * own_rows), 'dp')]
    unnamed x54 -> x9, local copies, waits for them, and re-layouts: 13.4 us -> 2.2 us
  transfers between devices with their start and end apart: 2 -> 0, of which waited for: 2 -> 0; matrix products, arithmetic and copies ran while one was open for 3% -> 0% of each run, Pallas kernels for 0% -> 0%
where the time goes in v1:
time: 76.9 us
  Pallas kernels  71.7 us (93%)
  local copies, waits for them, and re-layouts  4.1 us (5%)
  between operations  0.78 us (1%)
    pallas_call x1, Pallas kernels, fused(): pl.pallas_call(kernel, out_shape=jax.ShapeDtypeStruct((24, width), f32),...  71.7 us
    unnamed x9, local copies, waits for them, and re-layouts  2.2 us

profile of v1, /device:TPU:0, one launch (start us, length us, event | category | flops | bytes accessed | tf_op | source)
XLA Modules:
  0.0 76.9 jit_solution(12205136295025902976)
XLA Ops:
  0.7 0.1 broadcast_select_fusion
  0.8 1.1 %select_n.45 = bf16[4,4,2,24,2,4,128]{6,5,4,3,2,1,0:T(4,128)(2,1)S(1)} reshape(bf16[1,768,1024]{2,1,0:T(8,128)(2,1)S(1)} %broadcast_select_fusion) | data formatting | bytes 3145728 | tf_op jit(solution)/shard_map/jit(_where)/select_n | solution.py:302
  1.9 0.4 copy.9
  2.3 0.0 copy-start.3
  2.3 0.0 copy-start
  2.3 0.0 copy-start.2
  2.3 0.1 copy_bitcast_fusion.w_ref
  2.5 0.4 copy-done.3
  2.9 0.1 broadcast_in_dim.32
  3.0 0.1 select_n.39
  3.1 0.1 reshape.27
  3.2 0.0 copy-start.1
  3.2 0.2 pad_maximum_fusion.bias_ref
  3.4 0.1 copy-done
  3.5 0.0 copy-done.2
  3.6 1.0 %copy-done.1 = bf16[128,4096]{1,0:T(8,128)(2,1)S(1)} copy-done((bf16[128,4096]{1,0:T(8,128)(2,1)S(1)}, bf16[128,4096]{1,0:T(8,128)(2,1)}, u32[]{:S(2)}) %copy-start.1) | copy-done | bytes 1048600
  4.5 71.7 %shard_map.64 = f32[24,1024]{1,0:T(8,128)S(1)} custom-call(bf16[128,4096]{1,0:T(8,128)(2,1)S(1)} %copy-done, bf16[128,1024]{1,0:T(8,128)(2,1)S(1)} %copy-done.2, bf16[128,4096]{1,0:T(8,128)(2,1)S(1)} %copy-done.1, f32[896,256]{1,0:T(8,128)S(1)} %pad_maximum_fusion.bias_ref, bf16[4,2,4,2,2,48,128]{6,5,4,3,2,1,0:T(8,128)(2,1)S(1)} %copy_bitcast_fusion.w_ref), custom_call_target="tpu_custom_call" | custom-call | tf_op jit(solution)/shard_map/pallas_call | solution.py:314
  76.3 0.6 copy.14
  (5 shorter events, 0.0 us)
Async XLA Ops:
  2.3 0.7 copy-start.3
  2.3 1.2 %copy-start = (bf16[128,4096]{1,0:T(8,128)(2,1)S(1)}, bf16[128,4096]{1,0:T(8,128)(2,1)}, u32[]{:S(2)}) copy-start(bf16[128,4096]{1,0:T(8,128)(2,1)} %q_ref.1) | copy-start | bytes 3145732
  2.3 1.3 %copy-start.2 = (bf16[128,1024]{1,0:T(8,128)(2,1)S(1)}, bf16[128,1024]{1,0:T(8,128)(2,1)}, u32[]{:S(2)}) copy-start(bf16[128,1024]{1,0:T(8,128)(2,1)} %kv_ref.1) | copy-start | bytes 786436
  3.2 1.3 %copy-start.1 = (bf16[128,4096]{1,0:T(8,128)(2,1)S(1)}, bf16[128,4096]{1,0:T(8,128)(2,1)}, u32[]{:S(2)}) copy-start(bf16[128,4096]{1,0:T(8,128)(2,1)} %ct_ref.1) | copy-start | bytes 3145732

commit v2 on v1

--- a/solution.py
+++ b/solution.py
@@ -106,46 +106,66 @@
 LOG2E = 1.4426950408889634
 
 
-def attend(j, q_ref, kv_ref, ct_ref, bias_ref, cart, kk, vv, grad):
+PAIRS = 1
+SLICES = 2
+LAT = 2.2
+COST = 3.0
+
+
+def attend_begin(j, kv_ref, cart, kk, vv):
     slots = SLOTS_PER
     half = KVH * HD
     kk[:slots] = cart[j, :, :, :, 0].reshape(slots, HD)
     vv[:slots] = cart[j, :, :, :, 1].reshape(slots, HD)
     kk[slots:] = kv_ref[:, j * HD:(j + 1) * HD]
     vv[slots:] = kv_ref[:, half + j * HD:half + (j + 1) * HD]
+
+
+def attend_slice(j, part, q_ref, ct_ref, bias_ref, kk, vv, acc):
+    slots = SLOTS_PER
     groups = QH // KVH
-    grad[j] = jnp.zeros_like(grad[j])
-
-    def pair(i, carry):
-        base = j * groups * HD + i * 2 * HD
-        one = pl.ds(pl.multiple_of(base, HD), HD)
-        two = pl.ds(pl.multiple_of(base + HD, HD), HD)
-        q = jnp.concatenate([q_ref[:, one], q_ref[:, two]], axis=0)
-        ct = jnp.concatenate([ct_ref[:, one], ct_ref[:, two]], axis=0)
-        nt = (((1,), (1,)), ((), ()))
+    wide = groups // SLICES // PAIRS * HD
+    nt = (((1,), (1,)), ((), ()))
+    for i in range(PAIRS):
+        base = (j * groups) * HD + (part * PAIRS + i) * wide
+        cols = [slice(base + h, base + h + HD) for h in range(0, wide, HD)]
+        q = jnp.concatenate([q_ref[:, c] for c in cols], axis=0)
+        ct = jnp.concatenate([ct_ref[:, c] for c in cols], axis=0)
         scores = lax.dot_general(kk[...], q, nt, preferred_element_type=jnp.float32)
-        x = scores * (SCALE * LOG2E) + bias_ref[...]
+        x = scores * (SCALE * LOG2E) + bias_ref[:, :wide]
         e = jnp.exp2(x - jnp.max(x, axis=0, keepdims=True))
         prob = e * (1.0 / jnp.sum(e, axis=0, keepdims=True))
         low = prob.astype(jnp.bfloat16)
         gp = lax.dot_general(vv[...], ct, nt, preferred_element_type=jnp.float32)
         row_dot = jnp.sum(low.astype(jnp.float32) * gp, axis=0, keepdims=True)
         gs = (prob[:slots] * (gp[:slots] - row_dot)).astype(jnp.bfloat16)
-        grad[j, :, :HD] += jnp.dot(gs, q, preferred_element_type=jnp.float32)
-        grad[j, :, HD:] += jnp.dot(low[:slots], ct, preferred_element_type=jnp.float32)
-        return carry
-
-    lax.fori_loop(0, groups // 2, pair, 0)
-    grad[j, :, :HD] = grad[j, :, :HD] * SCALE
+        gk = jnp.dot(gs, q, preferred_element_type=jnp.float32)
+        gv = jnp.dot(low[:slots], ct, preferred_element_type=jnp.float32)
+        if part + i == 0:
+            acc[:, :HD] = gk
+            acc[:, HD:] = gv
+        else:
+            acc[:, :HD] += gk
+            acc[:, HD:] += gv
+
+
+def attend_end(j, acc, grad):
+    for z in range(4):
+        for xy in range(4):
+            for c in range(2):
+                row = 24 * ((z * 4 + xy) * 2 + c)
+                to = 24 * ((c * 4 + xy) * 4 + z)
+                grad[j, to:to + 24, :HD] = acc[row:row + 24, :HD] * SCALE
+                grad[j, to:to + 24, HD:] = acc[row:row + 24, HD:]
 
 
 SLOTS_PER = 768
 SEG = (24, 2 * HD)
-N_SEM = 21 * KVH + 7
-
-
-def kernel(q_ref, kv_ref, ct_ref, bias_ref, w_ref, out_ref,
-           cart, rc, a1, rx, a2, rz, kk, vv, grad,
+N_SEM = 21 * KVH + 10
+
+
+def kernel(q_hbm, kv_hbm, ct_hbm, own_cart, mask_ref, owner_ref, out_ref,
+           q_ref, kv_ref, ct_ref, load_sem, bias_ref, w_ref, acc, cart, rc, a1, rx, a2, rz, kk, vv, grad,
            gc, b1, sx, gx, b2, gz, own, sq, sqr, send_sem, recv_sem):
     me = lax.axis_index("dp")
     core = me % 2
@@ -169,11 +189,30 @@
     z_peer = {d: me + 8 * z_step[d] for d in (1, 2, 3)}
 
     barrier = pltpu.get_barrier_semaphore()
-    peers = [core_peer] + list(xy_peer.values()) + list(z_peer.values())
+    every = {d: me + moved(d % 2, 0) + 2 * moved(d // 2 % 4, 1) + 8 * moved(d // 8, 3) for d in range(1, 32)}
+    peers = [every[d] for d in range(1, 8)] + list(z_peer.values())
     for peer in peers:
         pl.semaphore_signal(barrier, inc=1, device_id={"dp": peer}, device_id_type=pl.DeviceIdType.MESH)
+
+    staged = [pltpu.make_async_copy(src, dst, load_sem.at[i])
+              for i, (src, dst) in enumerate([(q_hbm, q_ref), (ct_hbm, ct_ref), (kv_hbm, kv_ref)])]
+    for copy in staged:
+        copy.start()
+    mine = owner_ref[0] == me
+    for j in range(KVH):
+        for c in range(2):
+            for p in range(4):
+                for r in range(2):
+                    row = c * 384 + p * 96 + r * 48
+                    for v in range(2):
+                        col = (v * KVH + j) * HD
+                        w_ref[j, c, p, r, v] = jnp.where(mine, own_cart[0, row:row + 48, col:col + HD], 0).astype(jnp.bfloat16)
+    for u in range(0, SLOTS_PER, BLOCK):
+        bias_ref[u:u + BLOCK] = jnp.full((BLOCK, bias_ref.shape[1]), jnp.where(mask_ref[0, u // BLOCK] > 0, 0.0, masked_score), jnp.float32)
+    own_pos = lax.broadcasted_iota(jnp.int32, (BLOCK, bias_ref.shape[1]), 0)
+    row_pos = lax.broadcasted_iota(jnp.int32, (BLOCK, bias_ref.shape[1]), 1) % BLOCK
+    bias_ref[SLOTS_PER:] = jnp.where(own_pos <= row_pos, 0.0, masked_score)
     pl.semaphore_wait(barrier, len(peers))
-
     sent = []
     count = [0]
 
@@ -189,11 +228,11 @@
 
     def head(j):
         c = [send(w_ref.at[j, 1 - core], rc.at[j], core_peer)]
-        yield
+        yield ("c", 0.5)
         c[0].wait_recv()
         a1[j] = w_ref[j, core] + rc[j]
         c = [send(a1.at[j, xy + xy_step[d]], rx.at[j, d - 1], xy_peer[d]) for d in (1, 2, 3)]
-        yield
+        yield ("x", 2.0)
         for k in c:
             k.wait_recv()
         a2[j] = (a1[j, xy] + rx[j, 0]) + (rx[j, 1] + rx[j, 2])
@@ -201,35 +240,40 @@
         for d in (1, 2, 3):
             p = zz + z_step[d]
             c.append(send(a2.at[j, p // 2, p % 2], rz.at[j, d - 1], z_peer[d]))
-        yield
+        yield ("z", 1.0)
         for k in c:
             k.wait_recv()
         spot = cart.at[j, core, xy, zz // 2, zz % 2]
         cart[j, core, xy, zz // 2, zz % 2] = (a2[j, zz // 2, zz % 2] + rz[j, 0]) + (rz[j, 1] + rz[j, 2])
         c = [send(spot, spot, z_peer[d]) for d in (1, 2, 3)]
-        yield
+        yield ("z", 1.0)
         for k in c:
             k.wait_recv()
         spot = cart.at[j, core, xy]
         c = [send(spot, spot, xy_peer[d]) for d in (1, 2, 3)]
-        yield
+        yield ("x", 2.0)
         for k in c:
             k.wait_recv()
         c = [send(cart.at[j, core], cart.at[j, core], core_peer)]
-        yield
+        yield ("c", 0.5)
         c[0].wait_recv()
         yield "compute"
-        attend(j, q_ref, kv_ref, ct_ref, bias_ref, cart, kk, vv, grad)
+        attend_begin(j, kv_ref, cart, kk, vv)
+        for part in range(SLICES):
+            attend_slice(j, part, q_ref, ct_ref, bias_ref, kk, vv, acc)
+            if part < SLICES - 1:
+                yield "compute"
+        attend_end(j, acc, grad)
         half = SLOTS_PER // 2
         c = [send(grad.at[j, pl.ds(pl.multiple_of((1 - core) * half, 8), half)], gc.at[j], core_peer)]
-        yield
+        yield ("c", 0.8)
         c[0].wait_recv()
         b1[j] = (grad[j, pl.ds(pl.multiple_of(core * half, 8), half)] + gc[j]).reshape(4, half // 4, 2 * HD)
         c = []
         for d in (1, 2, 3):
             sx[j, d - 1] = b1[j, xy + xy_step[d]].astype(jnp.bfloat16)
             c.append(send(sx.at[j, d - 1], gx.at[j, d - 1], xy_peer[d]))
-        yield
+        yield ("x", 2.0)
         for k in c:
             k.wait_recv()
         total = b1[j, xy]
@@ -237,37 +281,43 @@
             total = total + gx[j, d - 1].astype(jnp.float32)
         b2[j] = total.reshape(4, SEG[0], SEG[1])
         c = [send(b2.at[j, zz + z_step[d]], gz.at[j, d - 1], z_peer[d]) for d in (1, 2, 3)]
-        yield
+        yield ("z", 2.0)
         for k in c:
             k.wait_recv()
         own[j] = (b2[j, zz] + gz[j, 0]) + (gz[j, 1] + gz[j, 2])
 
     heads = [head(j) for j in range(KVH)]
-    started = 0
-    waiting = {}
-    tick = 0
-    live = []
-    while True:
-        if started < KVH:
-            live.append(started)
-            started += 1
-        if not live:
-            break
-        ready = None
-        for j in list(live):
-            if j in waiting:
-                continue
-            try:
-                got = next(heads[j])
-                if got == "compute":
-                    waiting[j] = True
-            except StopIteration:
-                live.remove(j)
-        if waiting:
-            j = min(waiting)
-            del waiting[j]
-            next(heads[j])
-        tick += 1
+    link = {"c": 0.0, "x": 0.0, "z": 0.0}
+    now = 0.0
+    ready = {}
+    computing = []
+
+    def advance(j):
+        got = next(heads[j], None)
+        ready.pop(j, None)
+        if got == "compute":
+            computing.append(j)
+        elif got is not None:
+            name, cost = got
+            link[name] = max(link[name], now) + cost
+            ready[j] = link[name] + LAT
+
+    for j in range(KVH):
+        advance(j)
+    for copy in staged:
+        copy.wait()
+    while ready or computing:
+        arrived = [j for j in sorted(ready) if ready[j] <= now]
+        if arrived:
+            now += 0.15
+            advance(arrived[0])
+        elif computing:
+            j = min(computing)
+            computing.remove(j)
+            now += COST / SLICES
+            advance(j)
+        else:
+            now = min(ready.values())
 
     part = jnp.zeros((8, HD), jnp.float32)
     for j in range(KVH):
@@ -277,17 +327,15 @@
             for l in range(0, SEG[1], HD):
                 part = part + v[r:r + 8, l:l + HD]
     sq[0] = part
-    c = send(sq.at[0], sqr.at[0], core_peer)
-    c.wait_recv()
-    sq[1] = sq[0] + sqr[0]
-    cs = [send(sq.at[1], sqr.at[d], xy_peer[d]) for d in (1, 2, 3)]
+    eight = {d: every[d] for d in range(1, 8)}
+    cs = [send(sq.at[0], sqr.at[d - 1], eight[d]) for d in range(1, 8)]
     for k in cs:
         k.wait_recv()
-    sq[2] = (sq[1] + sqr[1]) + (sqr[2] + sqr[3])
-    cs = [send(sq.at[2], sqr.at[3 + d], z_peer[d]) for d in (1, 2, 3)]
+    sq[1] = (((sq[0] + sqr[0]) + (sqr[1] + sqr[2])) + ((sqr[3] + sqr[4]) + (sqr[5] + sqr[6])))
+    cs = [send(sq.at[1], sqr.at[6 + d], z_peer[d]) for d in (1, 2, 3)]
     for k in cs:
         k.wait_recv()
-    squares = jnp.sum((sq[2] + sqr[4]) + (sqr[5] + sqr[6]))
+    squares = jnp.sum((sq[1] + sqr[7]) + (sqr[8] + sqr[9]))
     factor = 1.0 / jnp.sqrt(squares * jnp.ones((1, HD), jnp.float32) / (SLOTS_PER * 2 * KVH * HD) + norm_epsilon)
     for j in range(KVH):
         out_ref[:, j * HD:(j + 1) * HD] = own[j, :, :HD] * factor
@@ -299,24 +347,23 @@
 def fused(queries, own_kv, cotangent, cartridges, block_mask, owner):
     slots, width = cartridges.shape[1:]
     seq = queries.shape[0]
-    mine = jnp.where(lax.axis_index("dp") == owner[0], cartridges[0], 0).astype(jnp.bfloat16)
-    w = mine.reshape(4, 4, 2, 24, 2, KVH, HD).transpose(5, 2, 1, 0, 3, 4, 6)
-    w = w.reshape(KVH, 2, 4, 2, 48, 2, HD).transpose(0, 1, 2, 3, 5, 4, 6)
-    allowed = jnp.repeat(block_mask[0] > 0, BLOCK)
-    allowed = allowed.reshape(4, 4, 2, 24).transpose(2, 1, 0, 3).reshape(slots)
-    bias = jnp.broadcast_to(jnp.where(allowed, 0.0, masked_score)[:, None], (slots, 2 * seq))
-    pos = jnp.arange(seq)
-    causal = jnp.where(pos[:, None] <= jnp.tile(pos, 2)[None, :], 0.0, masked_score)
-    bias = jnp.concatenate([bias, causal], axis=0).astype(jnp.float32)
     bf, f32 = jnp.bfloat16, jnp.float32
     vm = pl.BlockSpec(memory_space=pltpu.VMEM)
+    sm = pl.BlockSpec(memory_space=pltpu.SMEM)
     piece = (48, HD)
     return pl.pallas_call(
         kernel,
         out_shape=jax.ShapeDtypeStruct((24, width), f32),
-        in_specs=[vm] * 5,
+        in_specs=[pl.BlockSpec(memory_space=pl.ANY)] * 3 + [vm] + [sm] * 2,
         out_specs=vm,
         scratch_shapes=[
+            pltpu.VMEM(queries.shape, bf),
+            pltpu.VMEM(own_kv.shape, bf),
+            pltpu.VMEM(cotangent.shape, bf),
+            pltpu.SemaphoreType.DMA((3,)),
+            pltpu.VMEM((slots + seq, QH // KVH // SLICES // PAIRS * HD), f32),
+            pltpu.VMEM((KVH, 2, 4, 2, 2) + piece, bf),
+            pltpu.VMEM((slots, 2 * HD), f32),
             pltpu.VMEM((KVH, 2, 4, 2, 2) + piece, bf),
             pltpu.VMEM((KVH, 4, 2, 2) + piece, bf),
             pltpu.VMEM((KVH, 4, 2, 2) + piece, bf),
@@ -333,14 +380,14 @@
             pltpu.VMEM((KVH, 4) + SEG, f32),
             pltpu.VMEM((KVH, 3) + SEG, f32),
             pltpu.VMEM((KVH,) + SEG, f32),
-            pltpu.VMEM((3, 8, HD), f32),
-            pltpu.VMEM((7, 8, HD), f32),
+            pltpu.VMEM((2, 8, HD), f32),
+            pltpu.VMEM((10, 8, HD), f32),
             pltpu.SemaphoreType.DMA((N_SEM,)),
             pltpu.SemaphoreType.DMA((N_SEM,)),
         ],
         compiler_params=pltpu.CompilerParams(
             collective_id=0, has_side_effects=True, vmem_limit_bytes=48 * 1024 * 1024),
-    )(queries, own_kv, cotangent, bias, w)
+    )(queries, own_kv, cotangent, cartridges, block_mask, owner)
 
 
 def dispatch(size):

time: 76.9 us -> 69.3 us (0.901)
  Pallas kernels: 71.7 us -> 62.3 us
  local copies, waits for them, and re-layouts: 4.1 us -> 6.1 us
    pallas_call x1, Pallas kernels: 71.7 us -> 62.3 us  [fused(): pl.pallas_call(kernel, out_shape=jax.ShapeDtypeStruct((24, width), f32),...]
    unnamed x9 -> x11, local copies, waits for them, and re-layouts: 2.2 us -> 6.1 us
    select_n x4 -> x0, local copies, waits for them, and re-layouts: 1.32 us -> none  [the longest x1 1.13 us: fused(): jnp.where(lax.axis_index('dp') == owner[0], cartridges[0], 0)]
where the time goes in v2:
time: 69.3 us; the launch traced here: 69.1 us
  Pallas kernels  62.3 us (90%)
  local copies, waits for them, and re-layouts  6.1 us (9%)
    pallas_call x1, Pallas kernels, fused(): pl.pallas_call(kernel, out_shape=jax.ShapeDtypeStruct((24, width), f32),...  62.3 us
    unnamed x11, local copies, waits for them, and re-layouts  6.1 us

profile of v2, /device:TPU:0, one launch (start us, length us, event | category | flops | bytes accessed | tf_op | source)
XLA Modules:
  0.0 69.1 jit_solution(1022014698790412479)
XLA Ops:
  0.7 0.0 copy-start
  0.7 1.4 %copy-done = bf16[1,768,1024]{2,1,0:T(8,128)(2,1)S(1)} copy-done((bf16[1,768,1024]{2,1,0:T(8,128)(2,1)S(1)}, bf16[1,768,1024]{2,1,0:T(8,128)(2,1)}, u32[]{:S(2)}) %copy-start) | copy-done | bytes 1572888
  2.1 0.0 copy-start.1
  2.1 1.2 %copy-done.1 = bf16[128,4096]{1,0:T(8,128)(2,1)S(1)} copy-done((bf16[128,4096]{1,0:T(8,128)(2,1)S(1)}, bf16[128,4096]{1,0:T(8,128)(2,1)}, u32[]{:S(2)}) %copy-start.1) | copy-done | bytes 1048600
  3.3 0.0 copy-start.2
  3.3 1.2 %copy-done.2 = bf16[128,4096]{1,0:T(8,128)(2,1)S(1)} copy-done((bf16[128,4096]{1,0:T(8,128)(2,1)S(1)}, bf16[128,4096]{1,0:T(8,128)(2,1)}, u32[]{:S(2)}) %copy-start.2) | copy-done | bytes 1048600
  4.5 0.0 copy-start.3
  4.5 0.9 %copy-done.3 = bf16[128,1024]{1,0:T(8,128)(2,1)S(1)} copy-done((bf16[128,1024]{1,0:T(8,128)(2,1)S(1)}, bf16[128,1024]{1,0:T(8,128)(2,1)}, u32[]{:S(2)}) %copy-start.3) | copy-done | bytes 262168
  5.5 0.0 copy-start.4
  5.5 0.7 copy-done.4
  6.1 62.3 %shard_map.64 = f32[24,1024]{1,0:T(8,128)S(1)} custom-call(bf16[128,4096]{1,0:T(8,128)(2,1)S(1)} %copy-done.1, bf16[128,1024]{1,0:T(8,128)(2,1)S(1)} %copy-done.3, bf16[128,4096]{1,0:T(8,128)(2,1)S(1)} %copy-done.2, bf16[1,768,1024]{2,1,0:T(8,128)(2,1)S(1)} %copy-done, s32[1,6]{1,0:T(1,128)S(1)} %copy-done.4, s32[1]{0:T(128)S(6)} %copy.8.owner_ref), custom_call_target="tpu_custom_call" | custom-call | tf_op jit(solution)/shard_map/pallas_call | solution.py:354
  68.4 0.6 copy.9
Async XLA Ops:
  0.7 1.4 %copy-start = (bf16[1,768,1024]{2,1,0:T(8,128)(2,1)S(1)}, bf16[1,768,1024]{2,1,0:T(8,128)(2,1)}, u32[]{:S(2)}) copy-start(bf16[1,768,1024]{2,1,0:T(8,128)(2,1)} %own_cart.1) | copy-start | bytes 4718596
  2.1 1.2 %copy-start.1 = (bf16[128,4096]{1,0:T(8,128)(2,1)S(1)}, bf16[128,4096]{1,0:T(8,128)(2,1)}, u32[]{:S(2)}) copy-start(bf16[128,4096]{1,0:T(8,128)(2,1)} %q_hbm.1) | copy-start | bytes 3145732
  3.3 1.2 %copy-start.2 = (bf16[128,4096]{1,0:T(8,128)(2,1)S(1)}, bf16[128,4096]{1,0:T(8,128)(2,1)}, u32[]{:S(2)}) copy-start(bf16[128,4096]{1,0:T(8,128)(2,1)} %ct_hbm.1) | copy-start | bytes 3145732
  4.5 0.9 %copy-start.3 = (bf16[128,1024]{1,0:T(8,128)(2,1)S(1)}, bf16[128,1024]{1,0:T(8,128)(2,1)}, u32[]{:S(2)}) copy-start(bf16[128,1024]{1,0:T(8,128)(2,1)} %kv_hbm.1) | copy-start | bytes 786436
  5.5 0.7 copy-start.4

commit v3 on v2

--- a/solution.py
+++ b/solution.py
@@ -108,7 +108,7 @@
 
 PAIRS = 1
 SLICES = 2
-LAT = 2.2
+LAT = 1.8
 COST = 3.0
 
 
@@ -164,8 +164,8 @@
 N_SEM = 21 * KVH + 10
 
 
-def kernel(q_hbm, kv_hbm, ct_hbm, own_cart, mask_ref, owner_ref, out_ref,
-           q_ref, kv_ref, ct_ref, load_sem, bias_ref, w_ref, acc, cart, rc, a1, rx, a2, rz, kk, vv, grad,
+def kernel(q_hbm, kv_hbm, ct_hbm, cart_hbm, mask_ref, owner_ref, out_ref,
+           q_ref, kv_ref, ct_ref, own_cart, load_sem, bias_ref, w_ref, acc, cart, rc, a1, rx, a2, rz, kk, vv, grad,
            gc, b1, sx, gx, b2, gz, own, sq, sqr, send_sem, recv_sem):
     me = lax.axis_index("dp")
     core = me % 2
@@ -188,16 +188,22 @@
     xy_peer = {d: me + 2 * xy_step[d] for d in (1, 2, 3)}
     z_peer = {d: me + 8 * z_step[d] for d in (1, 2, 3)}
 
+    staged = [pltpu.make_async_copy(src, dst, load_sem.at[i])
+              for i, (src, dst) in enumerate([(cart_hbm, own_cart), (q_hbm, q_ref), (ct_hbm, ct_ref), (kv_hbm, kv_ref)])]
+    for copy in staged:
+        copy.start()
     barrier = pltpu.get_barrier_semaphore()
     every = {d: me + moved(d % 2, 0) + 2 * moved(d // 2 % 4, 1) + 8 * moved(d // 8, 3) for d in range(1, 32)}
     peers = [every[d] for d in range(1, 8)] + list(z_peer.values())
     for peer in peers:
         pl.semaphore_signal(barrier, inc=1, device_id={"dp": peer}, device_id_type=pl.DeviceIdType.MESH)
 
-    staged = [pltpu.make_async_copy(src, dst, load_sem.at[i])
-              for i, (src, dst) in enumerate([(q_hbm, q_ref), (ct_hbm, ct_ref), (kv_hbm, kv_ref)])]
-    for copy in staged:
-        copy.start()
+    for u in range(0, SLOTS_PER, BLOCK):
+        bias_ref[u:u + BLOCK] = jnp.full((BLOCK, bias_ref.shape[1]), jnp.where(mask_ref[0, u // BLOCK] > 0, 0.0, masked_score), jnp.float32)
+    own_pos = lax.broadcasted_iota(jnp.int32, (BLOCK, bias_ref.shape[1]), 0)
+    row_pos = lax.broadcasted_iota(jnp.int32, (BLOCK, bias_ref.shape[1]), 1) % BLOCK
+    bias_ref[SLOTS_PER:] = jnp.where(own_pos <= row_pos, 0.0, masked_score)
+    staged[0].wait()
     mine = owner_ref[0] == me
     for j in range(KVH):
         for c in range(2):
@@ -207,11 +213,6 @@
                     for v in range(2):
                         col = (v * KVH + j) * HD
                         w_ref[j, c, p, r, v] = jnp.where(mine, own_cart[0, row:row + 48, col:col + HD], 0).astype(jnp.bfloat16)
-    for u in range(0, SLOTS_PER, BLOCK):
-        bias_ref[u:u + BLOCK] = jnp.full((BLOCK, bias_ref.shape[1]), jnp.where(mask_ref[0, u // BLOCK] > 0, 0.0, masked_score), jnp.float32)
-    own_pos = lax.broadcasted_iota(jnp.int32, (BLOCK, bias_ref.shape[1]), 0)
-    row_pos = lax.broadcasted_iota(jnp.int32, (BLOCK, bias_ref.shape[1]), 1) % BLOCK
-    bias_ref[SLOTS_PER:] = jnp.where(own_pos <= row_pos, 0.0, masked_score)
     pl.semaphore_wait(barrier, len(peers))
     sent = []
     count = [0]
@@ -304,7 +305,7 @@
 
     for j in range(KVH):
         advance(j)
-    for copy in staged:
+    for copy in staged[1:]:
         copy.wait()
     while ready or computing:
         arrived = [j for j in sorted(ready) if ready[j] <= now]
@@ -354,13 +355,14 @@
     return pl.pallas_call(
         kernel,
         out_shape=jax.ShapeDtypeStruct((24, width), f32),
-        in_specs=[pl.BlockSpec(memory_space=pl.ANY)] * 3 + [vm] + [sm] * 2,
+        in_specs=[pl.BlockSpec(memory_space=pltpu.HBM)] * 4 + [sm] * 2,
         out_specs=vm,
         scratch_shapes=[
             pltpu.VMEM(queries.shape, bf),
             pltpu.VMEM(own_kv.shape, bf),
             pltpu.VMEM(cotangent.shape, bf),
-            pltpu.SemaphoreType.DMA((3,)),
+            pltpu.VMEM(cartridges.shape, bf),
+            pltpu.SemaphoreType.DMA((4,)),
             pltpu.VMEM((slots + seq, QH // KVH // SLICES // PAIRS * HD), f32),
             pltpu.VMEM((KVH, 2, 4, 2, 2) + piece, bf),
             pltpu.VMEM((slots, 2 * HD), f32),
@@ -386,7 +388,7 @@
             pltpu.SemaphoreType.DMA((N_SEM,)),
         ],
         compiler_params=pltpu.CompilerParams(
-            collective_id=0, has_side_effects=True, vmem_limit_bytes=48 * 1024 * 1024),
+            collective_id=0, has_side_effects=True, vmem_limit_bytes=62 * 1024 * 1024),
     )(queries, own_kv, cotangent, cartridges, block_mask, owner)
 
 

time: 69.3 us -> 65.4 us (0.944)
  local copies, waits for them, and re-layouts: 6.1 us -> 1.54 us
  Pallas kernels: 62.3 us -> 63.1 us
    unnamed x11 -> x1, local copies, waits for them, and re-layouts: 6.1 us -> 1.54 us
    pallas_call x1, Pallas kernels: 62.3 us -> 63.1 us  [fused(): pl.pallas_call(kernel, out_shape=jax.ShapeDtypeStruct((24, width), f32),...]
where the time goes in v3:
time: 65.4 us; the launch traced here: 65.3 us
  Pallas kernels  63.1 us (96%)
  local copies, waits for them, and re-layouts  1.54 us (2%)
  between operations  0.66 us (1%)
    pallas_call x1, Pallas kernels, fused(): pl.pallas_call(kernel, out_shape=jax.ShapeDtypeStruct((24, width), f32),...  63.1 us
    unnamed x1, local copies, waits for them, and re-layouts  1.54 us

profile of v3, /device:TPU:0, one launch (start us, length us, event | category | flops | bytes accessed | tf_op | source)
XLA Modules:
  0.0 65.3 jit_solution(8445041501350447895)
XLA Ops:
  0.7 63.1 %shard_map.64 = f32[24,1024]{1,0:T(8,128)} custom-call(bf16[128,4096]{1,0:T(8,128)(2,1)} %q_hbm.1, bf16[128,1024]{1,0:T(8,128)(2,1)} %kv_hbm.1, bf16[128,4096]{1,0:T(8,128)(2,1)} %ct_hbm.1, bf16[1,768,1024]{2,1,0:T(8,128)(2,1)} %cart_hbm.1, s32[1,6]{1,0:T(1,128)} %mask_ref.1, s32[1]{0:T(128)S(6)} %copy.8.owner_ref), custom_call_target="tpu_custom_call" | custom-call | tf_op jit(solution)/shard_map/pallas_call | solution.py:355
  63.7 1.5 %copy.9 = f32[24,1024]{1,0:T(8,128)} copy(f32[24,1024]{1,0:T(8,128)} %shard_map.64) | data formatting | bytes 196608
